TPU v7x, 512 devices: a whole 4x8x8 slice. The times are simulated.
512 devices in a mesh: row: 16 (over y_lo, x), col: 32 (over z, y_hi, core).
Axes of the slice: x: 4, y: 8 (y_hi: 2, y_lo: 4; y = y_hi * 4 + y_lo), z: 8, core: 2. Of those that a mesh axis runs over, the one named last changes fastest.
Arguments:
- gradient: bfloat16 [8192, 28672], P('row', 'col'), may hold values from -6 to 6
- projector: bfloat16 [8192, 1024], P(('row', 'col')), may hold values from -0.25 to 0.25
- first_moment: float32 [1024, 28672], P('row', 'col'), may hold values from -3 to 3
- second_moment: float32 [1024, 28672], P('row', 'col'), may hold values from 0.01 to 1
Outputs:
- update: float32 [8192, 28672], P('row', 'col')
- first_new: float32 [1024, 28672], P('row', 'col')
- second_new: float32 [1024, 28672], P('row', 'col')
All inputs are finite; a program needn't handle non-finite values.
Results may differ from a plain program's by a relative error of at most 0.0029.
Values may be sent and summed in bfloat16 or wider, within the bound.
A program may use at most 64 MiB of HBM per device.

v0:
```python
import jax
import jax.numpy as jnp
from jax import lax
from jax.sharding import PartitionSpec as P

beta_first = 0.9
beta_second = 0.999
epsilon = 1e-08


def project_rows(left_rows, right_rows):
    return lax.dot_general(
        left_rows, right_rows, (((0,), (0,)), ((), ())), preferred_element_type=jnp.float32
    )


def on_device(gradient, projector, first_moment, second_moment):
    gathered = lax.all_gather(projector, "col", axis=0, tiled=True)
    partial_value = project_rows(gathered, gradient)
    owned_share = lax.psum_scatter(partial_value, "row", scatter_dimension=0, tiled=True)
    first_new = beta_first * first_moment + (1.0 - beta_first) * owned_share
    second_new = beta_second * second_moment + (1.0 - beta_second) * owned_share * owned_share
    direction = (first_new / (jnp.sqrt(second_new) + epsilon)).astype(jnp.bfloat16)
    full_direction = lax.all_gather(direction, "row", axis=0, tiled=True)
    update = jnp.dot(gathered, full_direction, preferred_element_type=jnp.float32)
    return (update, first_new, second_new)


def solution(mesh):
    return jax.shard_map(
        on_device,
        mesh=mesh,
        in_specs=(P("row", "col"), P(("row", "col"), None), P("row", "col"), P("row", "col")),
        out_specs=(P("row", "col"), P("row", "col"), P("row", "col")),
        check_vma=False,
    )
```

profile of v0, /device:TPU:2, one launch (start us, length us, event | category | flops | bytes accessed | tf_op | source)
XLA Modules:
  0.0 292.6 jit_solution(4031112060552628608)
XLA Ops:
  7.2 0.0 copy-start
  7.2 0.0 all-gather.3.cloned.1.call-start
  7.2 0.7 all-gather.3.cloned.1.call-update
  7.9 0.0 reduce-scatter.2.cloned.1.call-start
  8.0 93.8 %all-gather.3.cloned.1.call-done = bf16[512,1024]{1,0:T(8,128)(2,1)} async-done(((bf16[16,1024]{1,0:T(8,128)(2,1)}), bf16[512,1024]{1,0:T(8,128)(2,1)}) %all-gather.3.cloned.1.call-update) | async-done | bytes 1048592 | tf_op jit(solution)/shard_map/all_gather | solution.py:18
  101.7 0.0 copy-done
  101.7 4.3 %fusion.2 = f32[1024,896]{1,0:T(8,128)} fusion(bf16[512,1024]{1,0:T(8,128)(2,1)} %all-gather.3.cloned.1.call-done, bf16[512,896]{1,0:T(8,128)(2,1)S(1)} %copy-done), kind=kOutput, calls=%fused_computation.5 | convolution fusion | flops 939524096 | bytes 5636096 | tf_op jit(solution)/shard_map/dot_general | solution.py:12
  106.0 0.0 copy-start.1
  106.0 0.0 copy-start.2
  106.0 0.0 reduce-scatter.2.cloned.1.call-update
  106.1 0.0 all-gather.5.cloned.1.call-start
  106.1 86.9 %reduce-scatter.2.cloned.1.call-done = f32[64,896]{1,0:T(8,128)} async-done(((f32[1024,896]{1,0:T(8,128)}), f32[64,896]{1,0:T(8,128)}) %reduce-scatter.2.cloned.1.call-update) | async-done | bytes 229392 | tf_op jit(solution)/shard_map/reduce_scatter | solution.py:20
  193.0 0.0 copy-done.1
  193.0 0.0 copy-done.2
  193.0 1.8 divide_convert_fusion
  194.8 0.0 all-gather.5.cloned.1.call-update
  194.8 86.6 %all-gather.5.cloned.1.call-done = bf16[1024,896]{1,0:T(8,128)(2,1)} async-done(((bf16[64,896]{1,0:T(8,128)(2,1)}), bf16[1024,896]{1,0:T(8,128)(2,1)}) %all-gather.5.cloned.1.call-update) | async-done | bytes 1835024 | tf_op jit(solution)/shard_map/all_gather | solution.py:24
  281.4 2.9 %convolution_bitcast_fusion = f32[512,896]{0,1:T(8,128)S(1)} fusion(bf16[1024,896]{1,0:T(8,128)(2,1)} %all-gather.5.cloned.1.call-done, bf16[512,1024]{1,0:T(8,128)(2,1)} %all-gather.3.cloned.1.call-done), kind=kOutput, calls=%fused_computation | convolution fusion | flops 939524096 | bytes 4718592 | tf_op jit(solution)/shard_map/dot_general | solution.py:25
  284.4 1.7 copy.7
Async XLA Ops:
  7.2 94.6 %copy-start = (bf16[512,896]{1,0:T(8,128)(2,1)S(1)}, bf16[512,896]{1,0:T(8,128)(2,1)}, u32[]{:S(2)}) copy-start(bf16[512,896]{1,0:T(8,128)(2,1)} %param.4) | copy-start | bytes 2752516
  7.2 94.5 %all-gather.3.cloned.1.call-start = ((), (), s32[]{:S(2)}) async-start(), calls=%async_computation.1 | async-start | bytes 1081344 | tf_op jit(solution)/shard_map/all_gather | solution.py:18
  7.9 185.1 %reduce-scatter.2.cloned.1.call-start = ((), (), s32[]{:S(2)}) async-start(), calls=%async_computation.2 | async-start | bytes 3899392 | tf_op jit(solution)/shard_map/reduce_scatter | solution.py:20
  106.0 87.0 %copy-start.1 = (f32[64,896]{1,0:T(8,128)S(1)}, f32[64,896]{1,0:T(8,128)}, u32[]{:S(2)}) copy-start(f32[64,896]{1,0:T(8,128)} %param.7) | copy-start | bytes 688132
  106.0 87.0 %copy-start.2 = (f32[64,896]{1,0:T(8,128)S(1)}, f32[64,896]{1,0:T(8,128)}, u32[]{:S(2)}) copy-start(f32[64,896]{1,0:T(8,128)} %param.6) | copy-start | bytes 688132
  106.1 175.4 %all-gather.5.cloned.1.call-start = ((), (), s32[]{:S(2)}) async-start(), calls=%async_computation.3 | async-start | bytes 1949696 | tf_op jit(solution)/shard_map/all_gather | solution.py:24
Sparse Core Ops, SparseCore 0:
  11.4 90.2 all-gather.2
  106.2 86.7 reduce-scatter.1
  195.7 85.7 all-gather.4
where the time goes:
time: 293 us
  waiting for transfers between devices  268 us (91%)
  between operations  13.8 us (5%)
  matrix products  7.25 us (2%)
    all_gather x1, waiting for transfers between devices, on_device(): gathered = lax.all_gather(projector, 'col', axis=0, tiled=True)  93.8 us
    reduce_scatter x1, waiting for transfers between devices, on_device(): lax.psum_scatter(partial_value, 'row', scatter_dimension=0, tiled=True)  86.9 us
    all_gather x1, waiting for transfers between devices, on_device(): full_direction = lax.all_gather(direction, 'row', axis=0, tiled=True)  86.6 us
  transfers between devices with their start and end apart: 3, of which 3 were waited for; matrix products, arithmetic and copies ran while one was open for 0% of the time, Pallas kernels for 0%

commit v1 on v0

v1 whole, which is shorter than its diff:
```python
import jax
import jax.numpy as jnp
from jax import lax
from jax.experimental import pallas as pl
from jax.experimental.pallas import tpu as pltpu
from jax.sharding import PartitionSpec as P

MESH = pl.DeviceIdType.MESH
beta_first = 0.9
beta_second = 0.999
epsilon = 1e-08

NX, NY, NZ = 4, 4, 8
CHUNK = 256
OWN = 64
COLS = 896
ROWS = 512


def kernel(
    grad, proj, mom1, mom2, update, first, second,
    pg, part, xs, xr, ys, yr, dirs,
    local_sem, ps_send, ps_recv, pf_send, pf_recv, sw_send, sw_recv,
    xs_sem, xr_sem, ys_sem, yr_sem, dx_send, dx_recv, dy_send, dy_recv,
):
    row = lax.axis_index("row")
    col = lax.axis_index("col")
    x, y = lax.rem(row, NX), lax.div(row, NX)
    k, h, z = lax.rem(col, 2), lax.rem(lax.div(col, 2), 2), lax.div(col, 4)
    zh = z * 2 + h

    def at_zh(dz, flip):
        other_z = lax.rem(z + dz, NZ)
        other_h = lax.rem(h + flip, 2)
        return (row, (other_z * 2 + other_h) * 2 + k)

    def at_x(d):
        return (y * NX + lax.rem(x + d, NX), col)

    def at_y(e):
        return (lax.rem(y + e, NY) * NX + x, col)

    other_core = (row, zh * 2 + 1 - k)

    def own_chunk(j):
        c = lax.rem(y + 1 + j, NY)
        return pltpu.make_async_copy(
            proj.at[:, pl.ds(pl.multiple_of(c * CHUNK, CHUNK), CHUNK)], pg.at[j, zh, k], local_sem.at[j]
        )

    for j in range(NY):
        own_chunk(j).start()

    barrier = pltpu.get_barrier_semaphore()

    @pl.loop(1, 16)
    def _(i):
        pl.semaphore_signal(barrier, inc=1, device_id=at_zh(lax.div(i, 2), lax.rem(i, 2)), device_id_type=MESH)

    @pl.loop(1, 4)
    def _(i):
        pl.semaphore_signal(barrier, inc=1, device_id=at_x(i), device_id_type=MESH)
        pl.semaphore_signal(barrier, inc=1, device_id=at_y(i), device_id_type=MESH)

    pl.semaphore_signal(barrier, inc=1, device_id=other_core, device_id_type=MESH)
    for j in range(NY):
        own_chunk(j).wait()
    pl.semaphore_wait(barrier, 22)

    def send_first(i):
        return pltpu.make_async_remote_copy(
            src_ref=pg.at[0, zh, k], dst_ref=pg.at[0, zh, k], send_sem=ps_send.at[i], recv_sem=ps_recv.at[i],
            device_id=at_zh(lax.div(i, 2), lax.rem(i, 2)), device_id_type=MESH)

    @pl.loop(0, 15)
    def _(i):
        send_first(15 - i).start()

    def send_rest(i, from_half):
        piece = pg.at[pl.ds(1, 3), z * 2 + lax.rem(h + from_half, 2), k]
        return pltpu.make_async_remote_copy(
            src_ref=piece, dst_ref=piece, send_sem=pf_send.at[from_half, i], recv_sem=pf_recv.at[from_half, i],
            device_id=at_zh(i, 0), device_id_type=MESH)

    def send_half():
        piece = pg.at[pl.ds(1, 3), zh, k]
        return pltpu.make_async_remote_copy(
            src_ref=piece, dst_ref=piece, send_sem=pf_send.at[0, 0], recv_sem=pf_recv.at[0, 0],
            device_id=at_zh(0, 1), device_id_type=MESH)

    send_half().start()

    @pl.loop(1, NZ)
    def _(i):
        send_rest(i, 0).start()

    def swap(first_chunk, count, s):
        piece = pg.at[pl.ds(first_chunk, count), :, k]
        return pltpu.make_async_remote_copy(
            src_ref=piece, dst_ref=piece, send_sem=sw_send.at[s], recv_sem=sw_recv.at[s],
            device_id=other_core, device_id_type=MESH)

    @pl.loop(1, 16)
    def _(i):
        send_first(i).wait_recv()

    swap(0, 1, 0).start()
    send_half().wait_recv()

    @pl.loop(1, NZ)
    def _(i):
        send_rest(i, 1).start()

    swap(0, 1, 0).wait_recv()

    def send_x(j, d):
        return pltpu.make_async_remote_copy(
            src_ref=xs.at[j, lax.rem(x + d, NX)], dst_ref=xr.at[j, d - 1], send_sem=xs_sem.at[j, d - 1],
            recv_sem=xr_sem.at[j, d - 1], device_id=at_x(d), device_id_type=MESH)

    def project(j):
        sums = lax.dot_general(
            pg[j].reshape(ROWS, CHUNK), grad[...], (((0,), (0,)), ((), ())), preferred_element_type=jnp.float32)
        sums = sums.reshape(NX, OWN, COLS)
        part[j] = sums
        xs[j] = sums.astype(jnp.bfloat16)
        for d in (2, 1, 3):
            send_x(j, d).start()

    def send_y(j):
        return pltpu.make_async_remote_copy(
            src_ref=ys.at[j], dst_ref=yr.at[j], send_sem=ys_sem.at[j], recv_sem=yr_sem.at[j],
            device_id=at_y(j + 1), device_id_type=MESH)

    def sum_x(j):
        total = part[j, x]
        for d in (1, 3, 2):
            send_x(j, d).wait_recv()
            total += xr[j, d - 1].astype(jnp.float32)
        return total

    project(0)

    @pl.loop(1, NZ)
    def _(i):
        send_rest(i, 0).wait_recv()
        send_rest(i, 1).wait_recv()

    swap(1, 3, 1).start()
    swap(1, 3, 1).wait_recv()

    @pl.loop(1, NY)
    def _(j):
        project(j)
        ys[j - 1] = sum_x(j - 1).astype(jnp.bfloat16)
        send_y(j - 1).start()

    lowrank = sum_x(3)
    for j in range(3):
        send_y(j).wait_recv()
        lowrank += yr[j].astype(jnp.float32)

    first_new = beta_first * mom1[...] + (1.0 - beta_first) * lowrank
    second_new = beta_second * mom2[...] + (1.0 - beta_second) * lowrank * lowrank
    dirs[3, x] = (first_new / (jnp.sqrt(second_new) + epsilon)).astype(jnp.bfloat16)

    def dir_y(e):
        return pltpu.make_async_remote_copy(
            src_ref=dirs.at[3, x], dst_ref=dirs.at[3 - e, x], send_sem=dy_send.at[e - 1], recv_sem=dy_recv.at[e - 1],
            device_id=at_y(e), device_id_type=MESH)

    def dir_x(s, d):
        return pltpu.make_async_remote_copy(
            src_ref=dirs.at[s, x], dst_ref=dirs.at[s, x], send_sem=dx_send.at[s, d - 1], recv_sem=dx_recv.at[s, d - 1],
            device_id=at_x(d), device_id_type=MESH)

    for e in (2, 1, 3):
        dir_y(e).start()
    for d in (2, 1, 3):
        dir_x(3, d).start()
    first[...] = first_new
    second[...] = second_new

    for e in (1, 3, 2):
        dir_y(e).wait_recv()
        for d in (2, 1, 3):
            dir_x(3 - e, d).start()

    def expand(s):
        for d in (1, 3, 2):
            dir_x(s, d).wait_recv()
        return jnp.dot(pg[s].reshape(ROWS, CHUNK), dirs[s].reshape(CHUNK, COLS), preferred_element_type=jnp.float32)

    update[...] = expand(3)
    for s in (2, 0, 1):
        update[...] += expand(s)

    @pl.loop(1, 16)
    def _(i):
        send_first(i).wait_send()

    send_half().wait_send()

    @pl.loop(1, NZ)
    def _(i):
        send_rest(i, 0).wait_send()
        send_rest(i, 1).wait_send()

    swap(0, 1, 0).wait_send()
    swap(1, 3, 1).wait_send()
    for d in (1, 2, 3):
        send_y(d - 1).wait_send()
        dir_y(d).wait_send()

        @pl.loop(0, NY)
        def _(j):
            send_x(j, d).wait_send()
            dir_x(j, d).wait_send()


def on_device(gradient, projector, first_moment, second_moment):
    vmem = pl.BlockSpec(memory_space=pltpu.VMEM)
    dma = pltpu.SemaphoreType.DMA
    return pl.pallas_call(
        kernel,
        out_shape=(
            jax.ShapeDtypeStruct((ROWS, COLS), jnp.float32),
            jax.ShapeDtypeStruct((OWN, COLS), jnp.float32),
            jax.ShapeDtypeStruct((OWN, COLS), jnp.float32),
        ),
        in_specs=[vmem, vmem, vmem, vmem],
        out_specs=(vmem, vmem, vmem),
        scratch_shapes=[
            pltpu.VMEM((NY, 16, 2, 16, CHUNK), jnp.bfloat16),
            pltpu.VMEM((NY, NX, OWN, COLS), jnp.float32),
            pltpu.VMEM((NY, NX, OWN, COLS), jnp.bfloat16),
            pltpu.VMEM((NY, 3, OWN, COLS), jnp.bfloat16),
            pltpu.VMEM((3, OWN, COLS), jnp.bfloat16),
            pltpu.VMEM((3, OWN, COLS), jnp.bfloat16),
            pltpu.VMEM((NY, NX, OWN, COLS), jnp.bfloat16),
            dma((4,)),
            dma((16,)), dma((16,)),
            dma((2, NZ)), dma((2, NZ)),
            dma((2,)), dma((2,)),
            dma((4, 3)), dma((4, 3)),
            dma((3,)), dma((3,)),
            dma((4, 3)), dma((4, 3)),
            dma((3,)), dma((3,)),
        ],
        compiler_params=pltpu.CompilerParams(
            collective_id=0, has_side_effects=True, vmem_limit_bytes=48 * 1024 * 1024
        ),
        cost_estimate=pl.CostEstimate(flops=4 * 512 * 1024 * 896, bytes_accessed=4 << 20, transcendentals=0),
    )(gradient, projector, first_moment, second_moment)


def solution(mesh):
    return jax.shard_map(
        on_device,
        mesh=mesh,
        in_specs=(P("row", "col"), P(("row", "col"), None), P("row", "col"), P("row", "col")),
        out_specs=(P("row", "col"), P("row", "col"), P("row", "col")),
        check_vma=False,
    )
```

time: 293 us -> 85.1 us (0.29)
  the two profiles are of different devices: /device:TPU:2 before, /device:TPU:18 now
where the time goes in v1:
time: 85.1 us; the launch traced here: 84.8 us
  Pallas kernels  77.7 us (91%)
  local copies, waits for them, and re-layouts  6.41 us (8%)
    pallas_call x1, Pallas kernels, on_device(): pl.pallas_call(kernel, out_shape=(jax.ShapeDtypeStruct((ROWS, COLS), jnp....  77.7 us
    unnamed x11, local copies, waits for them, and re-layouts  6.41 us

profile of v1, /device:TPU:18, one launch (start us, length us, event | category | flops | bytes accessed | tf_op | source)
XLA Modules:
  0.0 84.8 jit_solution(2133664438466153349)
XLA Ops:
  0.6 0.0 copy-start
  0.6 1.2 %copy-done = bf16[512,896]{1,0:T(8,128)(2,1)S(1)} copy-done((bf16[512,896]{1,0:T(8,128)(2,1)S(1)}, bf16[512,896]{1,0:T(8,128)(2,1)}, u32[]{:S(2)}) %copy-start) | copy-done | bytes 917528
  1.8 0.0 copy-start.1
  1.8 0.9 %copy-done.1 = f32[64,896]{1,0:T(8,128)S(1)} copy-done((f32[64,896]{1,0:T(8,128)S(1)}, f32[64,896]{1,0:T(8,128)}, u32[]{:S(2)}) %copy-start.1) | copy-done | bytes 229400
  2.8 0.0 copy-start.2
  2.8 0.9 %copy-done.2 = f32[64,896]{1,0:T(8,128)S(1)} copy-done((f32[64,896]{1,0:T(8,128)S(1)}, f32[64,896]{1,0:T(8,128)}, u32[]{:S(2)}) %copy-start.2) | copy-done | bytes 229400
  3.7 0.0 copy-start.3
  3.7 0.8 copy-done.3
  4.4 77.7 %shard_map.67 = (f32[512,896]{1,0:T(8,128)S(1)}, f32[64,896]{1,0:T(8,128)S(1)}, f32[64,896]{1,0:T(8,128)S(1)}) custom-call(bf16[512,896]{1,0:T(8,128)(2,1)S(1)} %copy-done, bf16[16,1024]{1,0:T(8,128)(2,1)S(1)} %copy-done.3, f32[64,896]{1,0:T(8,128)S(1)} %copy-done.1, f32[64,896]{1,0:T(8,128)S(1)} %copy-done.2), custom_call_target="tpu_custom_call" | custom-call | flops 1879048192 | bytes 4194304 | tf_op jit(solution)/shard_map/pallas_call | solution.py:224
  82.2 1.2 %copy.10 = f32[512,896]{1,0:T(8,128)} copy(f32[512,896]{1,0:T(8,128)S(1)} %get-tuple-element.6) | data formatting | bytes 3670016
  83.4 0.7 copy.11
  84.1 0.7 copy.12
Async XLA Ops:
  0.6 1.2 %copy-start = (bf16[512,896]{1,0:T(8,128)(2,1)S(1)}, bf16[512,896]{1,0:T(8,128)(2,1)}, u32[]{:S(2)}) copy-start(bf16[512,896]{1,0:T(8,128)(2,1)} %grad.1) | copy-start | bytes 2752516
  1.8 0.9 %copy-start.1 = (f32[64,896]{1,0:T(8,128)S(1)}, f32[64,896]{1,0:T(8,128)}, u32[]{:S(2)}) copy-start(f32[64,896]{1,0:T(8,128)} %mom1.1) | copy-start | bytes 688132
  2.8 0.9 %copy-start.2 = (f32[64,896]{1,0:T(8,128)S(1)}, f32[64,896]{1,0:T(8,128)}, u32[]{:S(2)}) copy-start(f32[64,896]{1,0:T(8,128)} %mom2.1) | copy-start | bytes 688132
  3.7 0.8 copy-start.3

commit v2 on v0

v2 whole, which is shorter than its diff:
```python
import jax
import jax.numpy as jnp
from jax import lax
from jax.experimental import pallas as pl
from jax.experimental.pallas import tpu as pltpu
from jax.sharding import PartitionSpec as P

MESH = pl.DeviceIdType.MESH
beta_first = 0.9
beta_second = 0.999
epsilon = 1e-08

NX, NY, NZ = 4, 4, 8
CHUNK = 256
OWN = 64
PART = 32
HALF = 16
COLS = 896
ROWS = 512


def kernel(
    grad_hbm, proj_hbm, mom1_hbm, mom2_hbm, update, first, second,
    grad, proj, mom1, mom2, pg, part, xs, ss, xr, ys, yr, dirs,
    local_sem, ps_send, ps_recv, hf_send, hf_recv, pf_send, pf_recv, sw_send, sw_recv,
    xs_sem, xr_sem, ys_sem, yr_sem, dx_send, dx_recv, dy_send, dy_recv,
):
    row = lax.axis_index("row")
    col = lax.axis_index("col")
    x, y = lax.rem(row, NX), lax.div(row, NX)
    k, h, z = lax.rem(col, 2), lax.rem(lax.div(col, 2), 2), lax.div(col, 4)
    zh = z * 2 + h

    def at_zh(dz, flip):
        other_z = lax.rem(z + dz, NZ)
        other_h = lax.rem(h + flip, 2)
        return (row, (other_z * 2 + other_h) * 2 + k)

    def x_of(d):
        return lax.rem(x + d, NX)

    def at_x(d):
        return (y * NX + x_of(d), col)

    def y_of(t):
        return lax.rem(lax.div(y, 2) + t // 2, 2) * 2 + lax.rem(lax.rem(y, 2) + t % 2, 2)

    def at_y(t):
        return (y_of(t) * NX + x, col)

    def remote(src, dst, send_sem, recv_sem, device):
        return pltpu.make_async_remote_copy(
            src_ref=src, dst_ref=dst, send_sem=send_sem, recv_sem=recv_sem, device_id=device, device_id_type=MESH)

    other_core = (row, zh * 2 + 1 - k)

    fetch_proj = pltpu.make_async_copy(proj_hbm, proj, local_sem.at[0])
    fetch_grad = pltpu.make_async_copy(grad_hbm, grad, local_sem.at[1])
    fetch_mom1 = pltpu.make_async_copy(mom1_hbm, mom1, local_sem.at[2])
    fetch_mom2 = pltpu.make_async_copy(mom2_hbm, mom2, local_sem.at[3])
    fetch_proj.start()

    barrier = pltpu.get_barrier_semaphore()

    @pl.loop(1, 16)
    def _(i):
        pl.semaphore_signal(barrier, inc=1, device_id=at_zh(lax.div(i, 2), lax.rem(i, 2)), device_id_type=MESH)

    for t in (1, 2, 3):
        pl.semaphore_signal(barrier, inc=1, device_id=at_y(t), device_id_type=MESH)
    for d in (1, 3):
        pl.semaphore_signal(barrier, inc=1, device_id=at_x(d), device_id_type=MESH)
    pl.semaphore_signal(barrier, inc=1, device_id=other_core, device_id_type=MESH)

    fetch_grad.start()
    fetch_mom1.start()
    fetch_mom2.start()
    fetch_proj.wait()

    for j in range(NY):
        owned = proj[:, pl.ds(pl.multiple_of(y_of(3 - j) * CHUNK, CHUNK), CHUNK)]
        for half in range(2):
            s = 4 * half + j
            picked = [owned[:, OWN * i + PART * half : OWN * i + PART * (half + 1)] for i in range(NX)]
            pg[s // 2, zh, k, :, pl.ds(s % 2 * 128, 128)] = jnp.concatenate(picked, axis=1)
    pl.semaphore_wait(barrier, 21)

    def send_first(i):
        piece = pg.at[0, zh, k]
        return remote(piece, piece, ps_send.at[i], ps_recv.at[i], at_zh(lax.div(i, 2), lax.rem(i, 2)))

    @pl.loop(0, 15)
    def _(i):
        send_first(15 - i).start()

    def send_half():
        piece = pg.at[pl.ds(1, 3), zh, k]
        return remote(piece, piece, hf_send, hf_recv, at_zh(0, 1))

    def send_rest(g, i, from_half):
        piece = pg.at[g, z * 2 + lax.rem(h + from_half, 2), k]
        return remote(piece, piece, pf_send.at[g - 1, from_half, i], pf_recv.at[g - 1, from_half, i], at_zh(i, 0))

    def send_rests(g, from_half):
        @pl.loop(1, NZ)
        def _(i):
            send_rest(g, lax.rem(i + 3, NZ - 1) + 1, from_half).start()

    def swap(g):
        piece = pg.at[g, :, k]
        return remote(piece, piece, sw_send.at[g], sw_recv.at[g], other_core)

    send_half().start()
    send_rests(1, 0)
    send_half().wait_recv()
    send_rests(1, 1)

    @pl.loop(1, 16)
    def _(i):
        send_first(i).wait_recv()

    swap(0).start()
    for g in (2, 3):
        send_rests(g, 0)
        send_rests(g, 1)
    fetch_grad.wait()
    swap(0).wait_recv()

    def rest_here(g):
        @pl.loop(1, NZ)
        def _(i):
            send_rest(g, i, 0).wait_recv()
            send_rest(g, i, 1).wait_recv()

        swap(g).start()

    low, high = pl.ds(0, HALF), pl.ds(HALF, HALF)

    def send_x(s, kind):
        src, d = (
            (xs.at[s, x_of(2), low], 1),
            (xs.at[s, x_of(2), high], 3),
            (xs.at[s, x_of(1), high], 1),
            (xs.at[s, x_of(3), low], 3),
            (ss.at[s, 0], 1),
            (ss.at[s, 1], 3),
        )[kind]
        return remote(src, xr.at[s, kind], xs_sem.at[s, kind], xr_sem.at[s, kind], at_x(d))

    def project(q):
        sums = lax.dot_general(
            pg[q].reshape(ROWS, CHUNK), grad[...], (((0,), (0,)), ((), ())), preferred_element_type=jnp.float32)
        sums = sums.reshape(2, NX, PART, COLS)
        part[pl.ds(2 * q, 2)] = sums
        xs[pl.ds(2 * q, 2)] = sums.astype(jnp.bfloat16)
        for kinds in ((0, 1), (2, 3)):
            for s in (2 * q, 2 * q + 1):
                for kind in kinds:
                    send_x(s, kind).start()

    def relay(s):
        send_x(s, 0).wait_recv()
        ss[s, 0] = (part[s, x_of(1), low] + xr[s, 0].astype(jnp.float32)).astype(jnp.bfloat16)
        send_x(s, 4).start()
        send_x(s, 1).wait_recv()
        ss[s, 1] = (part[s, x_of(3), high] + xr[s, 1].astype(jnp.float32)).astype(jnp.bfloat16)
        send_x(s, 5).start()

    def sum_x(s):
        for kind in range(2, 6):
            send_x(s, kind).wait_recv()
        lower = part[s, x, low] + xr[s, 3].astype(jnp.float32) + xr[s, 4].astype(jnp.float32)
        upper = part[s, x, high] + xr[s, 2].astype(jnp.float32) + xr[s, 5].astype(jnp.float32)
        return jnp.concatenate([lower, upper], axis=0)

    def send_y(s):
        return remote(ys.at[s], yr.at[s], ys_sem.at[s], yr_sem.at[s], at_y(3 - s % 4))

    def finish(s):
        ys[s] = sum_x(s).astype(jnp.bfloat16)
        send_y(s).start()

    def dir_y(half, t):
        own = 4 * half + 3
        return remote(dirs.at[own, x], dirs.at[own - t, x], dy_send.at[half, t - 1], dy_recv.at[half, t - 1], at_y(t))

    def dir_x(s, kind):
        src, d = (
            (dirs.at[s, x], 1),
            (dirs.at[s, x], 3),
            (dirs.at[s, x_of(3), low], 1),
            (dirs.at[s, x_of(1), high], 3),
        )[kind]
        return remote(src, src, dx_send.at[s, kind], dx_recv.at[s, kind], at_x(d))

    def spread(s):
        dir_x(s, 0).start()
        dir_x(s, 1).start()

    def spread_here(half, t):
        dir_y(half, t).wait_recv()
        spread(4 * half + 3 - t)

    def forward(s):
        for kind in range(2):
            dir_x(s, kind).wait_recv()
            dir_x(s, kind + 2).start()

    def expand(q):
        for s in (2 * q, 2 * q + 1):
            for kind in range(2, 4):
                dir_x(s, kind).wait_recv()
        return jnp.dot(
            pg[q].reshape(ROWS, CHUNK), dirs[pl.ds(2 * q, 2)].reshape(CHUNK, COLS), preferred_element_type=jnp.float32)

    def step(half):
        own = 4 * half + 3
        rows = pl.ds(PART * half, PART)
        lowrank = sum_x(own)
        for j in range(3):
            send_y(4 * half + j).wait_recv()
            lowrank += yr[4 * half + j].astype(jnp.float32)
        first_new = beta_first * mom1[rows] + (1.0 - beta_first) * lowrank
        second_new = beta_second * mom2[rows] + (1.0 - beta_second) * lowrank * lowrank
        dirs[own, x] = (first_new / (jnp.sqrt(second_new) + epsilon)).astype(jnp.bfloat16)
        for t in (3, 2, 1):
            dir_y(half, t).start()
        spread(own)
        first[rows] = first_new
        second[rows] = second_new

    project(0)
    rest_here(1)
    relay(0)
    relay(1)
    swap(1).wait_recv()
    project(1)
    rest_here(2)
    finish(0)
    finish(1)
    swap(2).wait_recv()
    relay(2)
    relay(3)
    project(2)
    rest_here(3)
    swap(3).wait_recv()
    project(3)
    finish(2)
    relay(4)
    relay(5)
    fetch_mom1.wait()
    fetch_mom2.wait()
    step(0)
    relay(6)
    relay(7)
    finish(4)
    finish(5)
    finish(6)
    spread_here(0, 1)
    forward(3)
    spread_here(0, 2)
    forward(2)
    step(1)
    spread_here(0, 3)
    forward(1)
    forward(0)
    update[...] = expand(1)

    @pl.loop(1, 16)
    def _(i):
        send_first(i).wait_send()

    send_half().wait_send()

    @pl.loop(1, NZ)
    def _(i):
        for g in (1, 2, 3):
            for from_half in range(2):
                send_rest(g, i, from_half).wait_send()

    for g in range(4):
        swap(g).wait_send()
    for s in (0, 1, 2, 4, 5, 6):
        send_y(s).wait_send()
    for s in range(8):
        for kind in range(6):
            send_x(s, kind).wait_send()

    spread_here(1, 1)
    forward(7)
    spread_here(1, 2)
    forward(6)
    update[...] += expand(0)
    spread_here(1, 3)
    forward(5)
    update[...] += expand(3)
    forward(4)
    for half in range(2):
        for t in (1, 2, 3):
            dir_y(half, t).wait_send()
    for s in (0, 1, 2, 3, 5, 6, 7):
        for kind in range(4):
            dir_x(s, kind).wait_send()
    update[...] += expand(2)
    for kind in range(4):
        dir_x(4, kind).wait_send()


def write_out(a_ref, b_ref, c_ref, a_out, b_out, c_out, sems):
    copies = [
        pltpu.make_async_copy(src, dst, sems.at[i])
        for i, (src, dst) in enumerate(((a_ref, a_out), (b_ref, b_out), (c_ref, c_out)))
    ]
    for copy in copies:
        copy.start()
    for copy in copies:
        copy.wait()


def on_device(gradient, projector, first_moment, second_moment):
    vmem = pl.BlockSpec(memory_space=pltpu.VMEM)
    hbm = pl.BlockSpec(memory_space=pltpu.HBM)
    dma = pltpu.SemaphoreType.DMA
    f32, bf16 = jnp.float32, jnp.bfloat16
    shapes = (
        jax.ShapeDtypeStruct((ROWS, COLS), f32),
        jax.ShapeDtypeStruct((OWN, COLS), f32),
        jax.ShapeDtypeStruct((OWN, COLS), f32),
    )
    results = pl.pallas_call(
        kernel,
        out_shape=shapes,
        in_specs=[hbm] * 4,
        out_specs=(vmem, vmem, vmem),
        scratch_shapes=[
            pltpu.VMEM((ROWS, COLS), bf16),
            pltpu.VMEM((16, 1024), bf16),
            pltpu.VMEM((OWN, COLS), f32),
            pltpu.VMEM((OWN, COLS), f32),
            pltpu.VMEM((4, 16, 2, 16, CHUNK), bf16),
            pltpu.VMEM((8, NX, PART, COLS), f32),
            pltpu.VMEM((8, NX, PART, COLS), bf16),
            pltpu.VMEM((8, 2, HALF, COLS), bf16),
            pltpu.VMEM((8, 6, HALF, COLS), bf16),
            pltpu.VMEM((8, PART, COLS), bf16),
            pltpu.VMEM((8, PART, COLS), bf16),
            pltpu.VMEM((8, NX, PART, COLS), bf16),
            dma((4,)),
            dma((16,)), dma((16,)),
            dma, dma,
            dma((3, 2, NZ)), dma((3, 2, NZ)),
            dma((4,)), dma((4,)),
            dma((8, 6)), dma((8, 6)),
            dma((8,)), dma((8,)),
            dma((8, 4)), dma((8, 4)),
            dma((2, 3)), dma((2, 3)),
        ],
        compiler_params=pltpu.CompilerParams(
            collective_id=0, has_side_effects=True, vmem_limit_bytes=60 * 1024 * 1024
        ),
        cost_estimate=pl.CostEstimate(flops=4 * 512 * 1024 * 896, bytes_accessed=4 << 20, transcendentals=0),
    )(gradient, projector, first_moment, second_moment)
    return pl.pallas_call(
        write_out,
        out_shape=shapes,
        in_specs=[vmem] * 3,
        out_specs=(hbm, hbm, hbm),
        scratch_shapes=[dma((3,))],
    )(*results)


def solution(mesh):
    return jax.shard_map(
        on_device,
        mesh=mesh,
        in_specs=(P("row", "col"), P(("row", "col"), None), P("row", "col"), P("row", "col")),
        out_specs=(P("row", "col"), P("row", "col"), P("row", "col")),
        check_vma=False,
    )
```

time: 293 us -> 75.5 us (0.26)
  waiting for transfers between devices: 268 us -> 0 us
  Pallas kernels: 0 us -> 74.7 us
  between operations: 13.8 us -> 0.64 us
  matrix products: 7.25 us -> 0 us
    all_gather x2 -> x0, waiting for transfers between devices: 180 us -> none  [the longest x1 93.8 us: on_device(): gathered = lax.all_gather(projector, 'col', axis=0, tiled=True)]
    reduce_scatter x1 -> x0, waiting for transfers between devices: 86.9 us -> none  [on_device(): lax.psum_scatter(partial_value, 'row', scatter_dimension=0, tiled=True)]
    pallas_call x0 -> x2, Pallas kernels: none -> 74.7 us  [the longest x1 71.7 us: on_device(): pl.pallas_call(kernel, out_shape=shapes, in_specs=[hbm] * 4, out_specs=(v...]
    dot_general x2 -> x0, matrix products: 7.25 us -> none  [the longest x1 4.32 us: project_rows(): lax.dot_general(left_rows, right_rows, (((0,), (0,)), ((), ())), preferre...]
  transfers between devices with their start and end apart: 3 -> 0, of which waited for: 3 -> 0; matrix products, arithmetic and copies ran while one was open for 0% -> 0% of each run, Pallas kernels for 0% -> 0%
where the time goes in v2:
time: 75.5 us; the launch traced here: 75.3 us
  Pallas kernels  74.7 us (99%)
    pallas_call x1, Pallas kernels, on_device(): pl.pallas_call(kernel, out_shape=shapes, in_specs=[hbm] * 4, out_specs=(v...  71.7 us
    pallas_call x1, Pallas kernels, on_device(): pl.pallas_call(write_out, out_shape=shapes, in_specs=[vmem] * 3, out_spec...  3.03 us

profile of v2, /device:TPU:2, one launch (start us, length us, event | category | flops | bytes accessed | tf_op | source)
XLA Modules:
  0.0 75.3 jit_solution(227909462813254593)
XLA Ops:
  0.6 71.7 %shard_map.67 = (f32[512,896]{1,0:T(8,128)}, f32[64,896]{1,0:T(8,128)}, f32[64,896]{1,0:T(8,128)}) custom-call(bf16[512,896]{1,0:T(8,128)(2,1)} %grad_hbm.1, bf16[16,1024]{1,0:T(8,128)(2,1)} %proj_hbm.1, f32[64,896]{1,0:T(8,128)} %mom1_hbm.1, f32[64,896]{1,0:T(8,128)} %mom2_hbm.1), custom_call_target="tpu_custom_call" | custom-call | flops 1879048192 | bytes 4194304 | tf_op jit(solution)/shard_map/pallas_call | solution.py:330
  72.3 3.0 %shard_map.68 = (f32[512,896]{1,0:T(8,128)}, f32[64,896]{1,0:T(8,128)}, f32[64,896]{1,0:T(8,128)}) custom-call(f32[512,896]{1,0:T(8,128)} %get-tuple-element.6.a_ref, f32[64,896]{1,0:T(8,128)} %get-tuple-element.7.b_ref, f32[64,896]{1,0:T(8,128)} %get-tuple-element.8.c_ref), custom_call_target="tpu_custom_call" | custom-call | tf_op jit(solution)/shard_map/pallas_call | solution.py:363

commit v3 on v2

--- a/solution.py
+++ b/solution.py
@@ -15,13 +15,16 @@
 OWN = 64
 PART = 32
 HALF = 16
+SUM_RELAYED = (0, 1, 2, 3, 4, 5, 6, 7)
+DIR_RELAYED = (0, 1, 2, 3, 4, 5, 6, 7)
+GROUPS = ((0, 1), (1, 1), (2, 2))
 COLS = 896
 ROWS = 512
 
 
 def kernel(
     grad_hbm, proj_hbm, mom1_hbm, mom2_hbm, update, first, second,
-    grad, proj, mom1, mom2, pg, part, xs, ss, xr, ys, yr, dirs,
+    grad, proj, mom1, mom2, pg, part, xs, ss, xr, xd, ys, yr, dirs,
     local_sem, ps_send, ps_recv, hf_send, hf_recv, pf_send, pf_recv, sw_send, sw_recv,
     xs_sem, xr_sem, ys_sem, yr_sem, dx_send, dx_recv, dy_send, dy_recv,
 ):
@@ -52,6 +55,9 @@
         return pltpu.make_async_remote_copy(
             src_ref=src, dst_ref=dst, send_sem=send_sem, recv_sem=recv_sem, device_id=device, device_id_type=MESH)
 
+    def wait_bytes(ref, sem):
+        pltpu.make_async_copy(ref, ref, sem).wait()
+
     other_core = (row, zh * 2 + 1 - k)
 
     fetch_proj = pltpu.make_async_copy(proj_hbm, proj, local_sem.at[0])
@@ -87,7 +93,7 @@
 
     def send_first(i):
         piece = pg.at[0, zh, k]
-        return remote(piece, piece, ps_send.at[i], ps_recv.at[i], at_zh(lax.div(i, 2), lax.rem(i, 2)))
+        return remote(piece, piece, ps_send, ps_recv, at_zh(lax.div(i, 2), lax.rem(i, 2)))
 
     @pl.loop(0, 15)
     def _(i):
@@ -98,8 +104,8 @@
         return remote(piece, piece, hf_send, hf_recv, at_zh(0, 1))
 
     def send_rest(g, i, from_half):
-        piece = pg.at[g, z * 2 + lax.rem(h + from_half, 2), k]
-        return remote(piece, piece, pf_send.at[g - 1, from_half, i], pf_recv.at[g - 1, from_half, i], at_zh(i, 0))
+        piece = pg.at[pl.ds(*GROUPS[g]), z * 2 + lax.rem(h + from_half, 2), k]
+        return remote(piece, piece, pf_send, pf_recv.at[g - 1], at_zh(i, 0))
 
     def send_rests(g, from_half):
         @pl.loop(1, NZ)
@@ -107,36 +113,32 @@
             send_rest(g, lax.rem(i + 3, NZ - 1) + 1, from_half).start()
 
     def swap(g):
-        piece = pg.at[g, :, k]
-        return remote(piece, piece, sw_send.at[g], sw_recv.at[g], other_core)
+        piece = pg.at[pl.ds(*GROUPS[g]), :, k]
+        return remote(piece, piece, sw_send, sw_recv.at[g], other_core)
 
     send_half().start()
     send_rests(1, 0)
     send_half().wait_recv()
     send_rests(1, 1)
-
-    @pl.loop(1, 16)
-    def _(i):
-        send_first(i).wait_recv()
-
+    send_rests(2, 0)
+    send_rests(2, 1)
+
+    wait_bytes(pg.at[0, pl.ds(0, 15), 0], ps_recv)
     swap(0).start()
-    for g in (2, 3):
-        send_rests(g, 0)
-        send_rests(g, 1)
     fetch_grad.wait()
     swap(0).wait_recv()
 
     def rest_here(g):
-        @pl.loop(1, NZ)
-        def _(i):
-            send_rest(g, i, 0).wait_recv()
-            send_rest(g, i, 1).wait_recv()
-
+        wait_bytes(pg.at[pl.ds(0, GROUPS[g][1]), pl.ds(0, 14), 0], pf_recv.at[g - 1])
         swap(g).start()
 
     low, high = pl.ds(0, HALF), pl.ds(HALF, HALF)
 
     def send_x(s, kind):
+        if s not in SUM_RELAYED:
+            d = (2, 1, 3)[kind]
+            return remote(
+                xs.at[s, x_of(d)], xd.at[s, kind], xs_sem.at[1], xr_sem.at[s, 0], at_x(d))
         src, d = (
             (xs.at[s, x_of(2), low], 1),
             (xs.at[s, x_of(2), high], 3),
@@ -145,7 +147,7 @@
             (ss.at[s, 0], 1),
             (ss.at[s, 1], 3),
         )[kind]
-        return remote(src, xr.at[s, kind], xs_sem.at[s, kind], xr_sem.at[s, kind], at_x(d))
+        return remote(src, xr.at[s, kind], xs_sem.at[0], xr_sem.at[s, kind], at_x(d))
 
     def project(q):
         sums = lax.dot_general(
@@ -156,9 +158,16 @@
         for kinds in ((0, 1), (2, 3)):
             for s in (2 * q, 2 * q + 1):
                 for kind in kinds:
+                    if s in SUM_RELAYED:
+                        send_x(s, kind).start()
+        for s in (2 * q, 2 * q + 1):
+            if s not in SUM_RELAYED:
+                for kind in range(3):
                     send_x(s, kind).start()
 
     def relay(s):
+        if s not in SUM_RELAYED:
+            return
         send_x(s, 0).wait_recv()
         ss[s, 0] = (part[s, x_of(1), low] + xr[s, 0].astype(jnp.float32)).astype(jnp.bfloat16)
         send_x(s, 4).start()
@@ -167,6 +176,12 @@
         send_x(s, 5).start()
 
     def sum_x(s):
+        if s not in SUM_RELAYED:
+            wait_bytes(xd.at[s], xr_sem.at[s, 0])
+            total = part[s, x]
+            for kind in range(3):
+                total += xd[s, kind].astype(jnp.float32)
+            return total
         for kind in range(2, 6):
             send_x(s, kind).wait_recv()
         lower = part[s, x, low] + xr[s, 3].astype(jnp.float32) + xr[s, 4].astype(jnp.float32)
@@ -174,7 +189,7 @@
         return jnp.concatenate([lower, upper], axis=0)
 
     def send_y(s):
-        return remote(ys.at[s], yr.at[s], ys_sem.at[s], yr_sem.at[s], at_y(3 - s % 4))
+        return remote(ys.at[s], yr.at[s], ys_sem, yr_sem.at[s], at_y(3 - s % 4))
 
     def finish(s):
         ys[s] = sum_x(s).astype(jnp.bfloat16)
@@ -182,34 +197,42 @@
 
     def dir_y(half, t):
         own = 4 * half + 3
-        return remote(dirs.at[own, x], dirs.at[own - t, x], dy_send.at[half, t - 1], dy_recv.at[half, t - 1], at_y(t))
+        return remote(dirs.at[own, x], dirs.at[own - t, x], dy_send, dy_recv.at[half, t - 1], at_y(t))
 
     def dir_x(s, kind):
+        if s not in DIR_RELAYED:
+            src, d = dirs.at[s, x], (2, 1, 3)[kind]
+            return remote(src, src, dx_send, dx_recv.at[s, 0], at_x(d))
         src, d = (
             (dirs.at[s, x], 1),
             (dirs.at[s, x], 3),
             (dirs.at[s, x_of(3), low], 1),
             (dirs.at[s, x_of(1), high], 3),
         )[kind]
-        return remote(src, src, dx_send.at[s, kind], dx_recv.at[s, kind], at_x(d))
+        return remote(src, src, dx_send, dx_recv.at[s, kind], at_x(d))
 
     def spread(s):
-        dir_x(s, 0).start()
-        dir_x(s, 1).start()
+        for kind in range(2 if s in DIR_RELAYED else 3):
+            dir_x(s, kind).start()
 
     def spread_here(half, t):
         dir_y(half, t).wait_recv()
         spread(4 * half + 3 - t)
 
     def forward(s):
+        if s not in DIR_RELAYED:
+            return
         for kind in range(2):
             dir_x(s, kind).wait_recv()
             dir_x(s, kind + 2).start()
 
     def expand(q):
         for s in (2 * q, 2 * q + 1):
-            for kind in range(2, 4):
-                dir_x(s, kind).wait_recv()
+            if s in DIR_RELAYED:
+                for kind in range(2, 4):
+                    dir_x(s, kind).wait_recv()
+            else:
+                wait_bytes(dirs.at[s, pl.ds(0, 3)], dx_recv.at[s, 0])
         return jnp.dot(
             pg[q].reshape(ROWS, CHUNK), dirs[pl.ds(2 * q, 2)].reshape(CHUNK, COLS), preferred_element_type=jnp.float32)
 
@@ -223,7 +246,7 @@
         first_new = beta_first * mom1[rows] + (1.0 - beta_first) * lowrank
         second_new = beta_second * mom2[rows] + (1.0 - beta_second) * lowrank * lowrank
         dirs[own, x] = (first_new / (jnp.sqrt(second_new) + epsilon)).astype(jnp.bfloat16)
-        for t in (3, 2, 1):
+        for t in (1, 2, 3):
             dir_y(half, t).start()
         spread(own)
         first[rows] = first_new
@@ -235,75 +258,56 @@
     relay(1)
     swap(1).wait_recv()
     project(1)
-    rest_here(2)
     finish(0)
     finish(1)
-    swap(2).wait_recv()
+    rest_here(2)
     relay(2)
     relay(3)
+    swap(2).wait_recv()
     project(2)
-    rest_here(3)
-    swap(3).wait_recv()
     project(3)
     finish(2)
+    fetch_mom1.wait()
+    fetch_mom2.wait()
     relay(4)
     relay(5)
-    fetch_mom1.wait()
-    fetch_mom2.wait()
     step(0)
     relay(6)
     relay(7)
     finish(4)
     finish(5)
+    spread_here(0, 1)
     finish(6)
-    spread_here(0, 1)
     forward(3)
     spread_here(0, 2)
-    forward(2)
     step(1)
     spread_here(0, 3)
+    forward(2)
     forward(1)
+    spread_here(1, 1)
     forward(0)
-    update[...] = expand(1)
-
-    @pl.loop(1, 16)
-    def _(i):
-        send_first(i).wait_send()
-
-    send_half().wait_send()
-
-    @pl.loop(1, NZ)
-    def _(i):
-        for g in (1, 2, 3):
-            for from_half in range(2):
-                send_rest(g, i, from_half).wait_send()
-
-    for g in range(4):
-        swap(g).wait_send()
-    for s in (0, 1, 2, 4, 5, 6):
-        send_y(s).wait_send()
-    for s in range(8):
-        for kind in range(6):
-            send_x(s, kind).wait_send()
-
-    spread_here(1, 1)
     forward(7)
     spread_here(1, 2)
+    update[...] = expand(1)
+    spread_here(1, 3)
     forward(6)
+    forward(5)
     update[...] += expand(0)
-    spread_here(1, 3)
-    forward(5)
+    forward(4)
     update[...] += expand(3)
-    forward(4)
-    for half in range(2):
-        for t in (1, 2, 3):
-            dir_y(half, t).wait_send()
-    for s in (0, 1, 2, 3, 5, 6, 7):
-        for kind in range(4):
-            dir_x(s, kind).wait_send()
     update[...] += expand(2)
-    for kind in range(4):
-        dir_x(4, kind).wait_send()
+
+    wait_bytes(pg.at[0, pl.ds(0, 15), 0], ps_send)
+    send_half().wait_send()
+    wait_bytes(pg.at[pl.ds(0, 3), pl.ds(0, 14), 0], pf_send)
+    wait_bytes(pg.at[:, :, 0], sw_send)
+    wait_bytes(ys.at[pl.ds(0, 6)], ys_sem)
+    if SUM_RELAYED:
+        wait_bytes(xr.at[pl.ds(0, len(SUM_RELAYED))], xs_sem.at[0])
+    if len(SUM_RELAYED) < 8:
+        wait_bytes(xd.at[pl.ds(0, 8 - len(SUM_RELAYED))], xs_sem.at[1])
+    wait_bytes(dirs.at[pl.ds(0, 2), pl.ds(0, 3)], dy_send)
+    wait_bytes(dirs.at[:, pl.ds(0, 3)], dx_send)
 
 
 def write_out(a_ref, b_ref, c_ref, a_out, b_out, c_out, sems):
@@ -342,30 +346,32 @@
             pltpu.VMEM((8, NX, PART, COLS), bf16),
             pltpu.VMEM((8, 2, HALF, COLS), bf16),
             pltpu.VMEM((8, 6, HALF, COLS), bf16),
+            pltpu.VMEM((8, 3, PART, COLS), bf16),
             pltpu.VMEM((8, PART, COLS), bf16),
             pltpu.VMEM((8, PART, COLS), bf16),
             pltpu.VMEM((8, NX, PART, COLS), bf16),
             dma((4,)),
-            dma((16,)), dma((16,)),
             dma, dma,
-            dma((3, 2, NZ)), dma((3, 2, NZ)),
-            dma((4,)), dma((4,)),
-            dma((8, 6)), dma((8, 6)),
-            dma((8,)), dma((8,)),
-            dma((8, 4)), dma((8, 4)),
-            dma((2, 3)), dma((2, 3)),
+            dma, dma,
+            dma, dma((2,)),
+            dma, dma((3,)),
+            dma((2,)), dma((8, 6)),
+            dma, dma((8,)),
+            dma, dma((8, 4)),
+            dma, dma((2, 3)),
         ],
         compiler_params=pltpu.CompilerParams(
-            collective_id=0, has_side_effects=True, vmem_limit_bytes=60 * 1024 * 1024
+            collective_id=0, has_side_effects=True, vmem_limit_bytes=40 * 1024 * 1024
         ),
         cost_estimate=pl.CostEstimate(flops=4 * 512 * 1024 * 896, bytes_accessed=4 << 20, transcendentals=0),
-    )(gradient, projector, first_moment, second_moment)
+    )(*[pltpu.with_memory_space_constraint(a, pltpu.HBM) for a in (gradient, projector, first_moment, second_moment)])
     return pl.pallas_call(
         write_out,
         out_shape=shapes,
         in_specs=[vmem] * 3,
         out_specs=(hbm, hbm, hbm),
         scratch_shapes=[dma((3,))],
+        compiler_params=pltpu.CompilerParams(vmem_limit_bytes=8 * 1024 * 1024),
     )(*results)
 
 

time: 75.5 us -> 68.4 us (0.906)
  the two profiles are of different devices: /device:TPU:2 before, /device:TPU:64 now
where the time goes in v3:
time: 68.4 us; the launch traced here: 68.2 us
  Pallas kernels  67.6 us (99%)
    pallas_call x1, Pallas kernels, on_device(): pl.pallas_call(kernel, out_shape=shapes, in_specs=[hbm] * 4, out_specs=(v...  66.2 us
    pallas_call x1, Pallas kernels, on_device(): pl.pallas_call(write_out, out_shape=shapes, in_specs=[vmem] * 3, out_spec...  1.4 us

profile of v3, /device:TPU:64, one launch (start us, length us, event | category | flops | bytes accessed | tf_op | source)
XLA Modules:
  0.0 68.2 jit_solution(2288756934496669577)
XLA Ops:
  0.6 66.2 %shard_map.67 = (f32[512,896]{1,0:T(8,128)S(1)}, f32[64,896]{1,0:T(8,128)S(1)}, f32[64,896]{1,0:T(8,128)S(1)}) custom-call(bf16[512,896]{1,0:T(8,128)(2,1)} %grad_hbm.1, bf16[16,1024]{1,0:T(8,128)(2,1)} %proj_hbm.1, f32[64,896]{1,0:T(8,128)} %mom1_hbm.1, f32[64,896]{1,0:T(8,128)} %mom2_hbm.1), custom_call_target="tpu_custom_call" | custom-call | flops 1879048192 | bytes 4194304 | tf_op jit(solution)/shard_map/pallas_call | solution.py:334
  66.8 1.4 %shard_map.68 = (f32[512,896]{1,0:T(8,128)}, f32[64,896]{1,0:T(8,128)}, f32[64,896]{1,0:T(8,128)}) custom-call(f32[512,896]{1,0:T(8,128)S(1)} %get-tuple-element.6.a_ref, f32[64,896]{1,0:T(8,128)S(1)} %get-tuple-element.7.b_ref, f32[64,896]{1,0:T(8,128)S(1)} %get-tuple-element.8.c_ref), custom_call_target="tpu_custom_call" | custom-call | tf_op jit(solution)/shard_map/pallas_call | solution.py:368

commit v4 on v3

--- a/solution.py
+++ b/solution.py
@@ -97,7 +97,7 @@
 
     @pl.loop(0, 15)
     def _(i):
-        send_first(15 - i).start()
+        send_first(i + 1).start()
 
     def send_half():
         piece = pg.at[pl.ds(1, 3), zh, k]
@@ -278,18 +278,18 @@
     finish(5)
     spread_here(0, 1)
     finish(6)
+    spread_here(0, 2)
     forward(3)
-    spread_here(0, 2)
+    spread_here(0, 3)
     step(1)
-    spread_here(0, 3)
     forward(2)
     forward(1)
     spread_here(1, 1)
     forward(0)
     forward(7)
     spread_here(1, 2)
+    spread_here(1, 3)
     update[...] = expand(1)
-    spread_here(1, 3)
     forward(6)
     forward(5)
     update[...] += expand(0)

time: 68.4 us -> 67.5 us (0.987)
  the two profiles are of different devices: /device:TPU:64 before, /device:TPU:58 now
where the time goes in v4:
time: 67.5 us; the launch traced here: 67.3 us
  Pallas kernels  66.7 us (99%)
    pallas_call x1, Pallas kernels, on_device(): pl.pallas_call(kernel, out_shape=shapes, in_specs=[hbm] * 4, out_specs=(v...  65.3 us
    pallas_call x1, Pallas kernels, on_device(): pl.pallas_call(write_out, out_shape=shapes, in_specs=[vmem] * 3, out_spec...  1.4 us

profile of v4, /device:TPU:58, one launch (start us, length us, event | category | flops | bytes accessed | tf_op | source)
XLA Modules:
  0.0 67.3 jit_solution(15428051548935496551)
XLA Ops:
  0.6 65.3 %shard_map.67 = (f32[512,896]{1,0:T(8,128)S(1)}, f32[64,896]{1,0:T(8,128)S(1)}, f32[64,896]{1,0:T(8,128)S(1)}) custom-call(bf16[512,896]{1,0:T(8,128)(2,1)} %grad_hbm.1, bf16[16,1024]{1,0:T(8,128)(2,1)} %proj_hbm.1, f32[64,896]{1,0:T(8,128)} %mom1_hbm.1, f32[64,896]{1,0:T(8,128)} %mom2_hbm.1), custom_call_target="tpu_custom_call" | custom-call | flops 1879048192 | bytes 4194304 | tf_op jit(solution)/shard_map/pallas_call | solution.py:334
  65.9 1.4 %shard_map.68 = (f32[512,896]{1,0:T(8,128)}, f32[64,896]{1,0:T(8,128)}, f32[64,896]{1,0:T(8,128)}) custom-call(f32[512,896]{1,0:T(8,128)S(1)} %get-tuple-element.6.a_ref, f32[64,896]{1,0:T(8,128)S(1)} %get-tuple-element.7.b_ref, f32[64,896]{1,0:T(8,128)S(1)} %get-tuple-element.8.c_ref), custom_call_target="tpu_custom_call" | custom-call | tf_op jit(solution)/shard_map/pallas_call | solution.py:368

commit v5 on v4

--- a/solution.py
+++ b/solution.py
@@ -120,11 +120,10 @@
     send_rests(1, 0)
     send_half().wait_recv()
     send_rests(1, 1)
-    send_rests(2, 0)
-    send_rests(2, 1)
 
     wait_bytes(pg.at[0, pl.ds(0, 15), 0], ps_recv)
     swap(0).start()
+    send_rests(2, 0)
     fetch_grad.wait()
     swap(0).wait_recv()
 
@@ -253,6 +252,7 @@
         second[rows] = second_new
 
     project(0)
+    send_rests(2, 1)
     rest_here(1)
     relay(0)
     relay(1)
@@ -275,8 +275,8 @@
     relay(6)
     relay(7)
     finish(4)
+    spread_here(0, 1)
     finish(5)
-    spread_here(0, 1)
     finish(6)
     spread_here(0, 2)
     forward(3)
@@ -295,7 +295,6 @@
     update[...] += expand(0)
     forward(4)
     update[...] += expand(3)
-    update[...] += expand(2)
 
     wait_bytes(pg.at[0, pl.ds(0, 15), 0], ps_send)
     send_half().wait_send()
@@ -308,6 +307,7 @@
         wait_bytes(xd.at[pl.ds(0, 8 - len(SUM_RELAYED))], xs_sem.at[1])
     wait_bytes(dirs.at[pl.ds(0, 2), pl.ds(0, 3)], dy_send)
     wait_bytes(dirs.at[:, pl.ds(0, 3)], dx_send)
+    update[...] += expand(2)
 
 
 def write_out(a_ref, b_ref, c_ref, a_out, b_out, c_out, sems):

time: 67.5 us -> 67.3 us (level)
  no operation moved by 1% of the time
where the time goes in v5:
time: 67.3 us; the launch traced here: 67.2 us
  Pallas kernels  66.5 us (99%)
    pallas_call x1, Pallas kernels, on_device(): pl.pallas_call(kernel, out_shape=shapes, in_specs=[hbm] * 4, out_specs=(v...  65.1 us
    pallas_call x1, Pallas kernels, on_device(): pl.pallas_call(write_out, out_shape=shapes, in_specs=[vmem] * 3, out_spec...  1.4 us

profile of v5, /device:TPU:58, one launch (start us, length us, event | category | flops | bytes accessed | tf_op | source)
XLA Modules:
  0.0 67.2 jit_solution(16829459384626677995)
XLA Ops:
  0.6 65.1 %shard_map.67 = (f32[512,896]{1,0:T(8,128)S(1)}, f32[64,896]{1,0:T(8,128)S(1)}, f32[64,896]{1,0:T(8,128)S(1)}) custom-call(bf16[512,896]{1,0:T(8,128)(2,1)} %grad_hbm.1, bf16[16,1024]{1,0:T(8,128)(2,1)} %proj_hbm.1, f32[64,896]{1,0:T(8,128)} %mom1_hbm.1, f32[64,896]{1,0:T(8,128)} %mom2_hbm.1), custom_call_target="tpu_custom_call" | custom-call | flops 1879048192 | bytes 4194304 | tf_op jit(solution)/shard_map/pallas_call | solution.py:334
  65.8 1.4 %shard_map.68 = (f32[512,896]{1,0:T(8,128)}, f32[64,896]{1,0:T(8,128)}, f32[64,896]{1,0:T(8,128)}) custom-call(f32[512,896]{1,0:T(8,128)S(1)} %get-tuple-element.6.a_ref, f32[64,896]{1,0:T(8,128)S(1)} %get-tuple-element.7.b_ref, f32[64,896]{1,0:T(8,128)S(1)} %get-tuple-element.8.c_ref), custom_call_target="tpu_custom_call" | custom-call | tf_op jit(solution)/shard_map/pallas_call | solution.py:368

commit v6 on v5

--- a/solution.py
+++ b/solution.py
@@ -289,11 +289,11 @@
     forward(7)
     spread_here(1, 2)
     spread_here(1, 3)
-    update[...] = expand(1)
     forward(6)
     forward(5)
+    update[...] = expand(1)
+    forward(4)
     update[...] += expand(0)
-    forward(4)
     update[...] += expand(3)
 
     wait_bytes(pg.at[0, pl.ds(0, 15), 0], ps_send)

time: 67.3 us -> 67.3 us (level)
  no operation moved by 1% of the time
where the time goes in v6:
time: 67.3 us; the launch traced here: 67.2 us
  Pallas kernels  66.5 us (99%)
    pallas_call x1, Pallas kernels, on_device(): pl.pallas_call(kernel, out_shape=shapes, in_specs=[hbm] * 4, out_specs=(v...  65.1 us
    pallas_call x1, Pallas kernels, on_device(): pl.pallas_call(write_out, out_shape=shapes, in_specs=[vmem] * 3, out_spec...  1.4 us

profile of v6, /device:TPU:58, one launch (start us, length us, event | category | flops | bytes accessed | tf_op | source)
XLA Modules:
  0.0 67.2 jit_solution(8430988194647254175)
XLA Ops:
  0.6 65.1 %shard_map.67 = (f32[512,896]{1,0:T(8,128)S(1)}, f32[64,896]{1,0:T(8,128)S(1)}, f32[64,896]{1,0:T(8,128)S(1)}) custom-call(bf16[512,896]{1,0:T(8,128)(2,1)} %grad_hbm.1, bf16[16,1024]{1,0:T(8,128)(2,1)} %proj_hbm.1, f32[64,896]{1,0:T(8,128)} %mom1_hbm.1, f32[64,896]{1,0:T(8,128)} %mom2_hbm.1), custom_call_target="tpu_custom_call" | custom-call | flops 1879048192 | bytes 4194304 | tf_op jit(solution)/shard_map/pallas_call | solution.py:334
  65.8 1.4 %shard_map.68 = (f32[512,896]{1,0:T(8,128)}, f32[64,896]{1,0:T(8,128)}, f32[64,896]{1,0:T(8,128)}) custom-call(f32[512,896]{1,0:T(8,128)S(1)} %get-tuple-element.6.a_ref, f32[64,896]{1,0:T(8,128)S(1)} %get-tuple-element.7.b_ref, f32[64,896]{1,0:T(8,128)S(1)} %get-tuple-element.8.c_ref), custom_call_target="tpu_custom_call" | custom-call | tf_op jit(solution)/shard_map/pallas_call | solution.py:368
